TPU v7x, 32 devices: a whole 2x2x4 slice. The times are simulated.
32 devices in a mesh: groups: 2 (over y), context: 4 (over z), tensor: 4 (over x, core).
Axes of the slice: x: 2, y: 2, z: 4, core: 2. Of those that a mesh axis runs over, the one named last changes fastest.
Arguments:
- inputs: bfloat16 [4096, 1024], P(('groups', 'context')), parts along dimension 0, may hold values from -6 to 6
- frame_valid: int32 [4096], P(('groups', 'context')), parts along dimension 0, may hold values from 0 to 1, as said below
- norm1_gain: float32 [1024], replicated, may hold values from 0.1 to 1.9
- w_query: bfloat16 [1024, 1024], P(None, 'tensor')
- w_key: bfloat16 [1024, 1024], P(None, 'tensor')
- w_value: bfloat16 [1024, 1024], P(None, 'tensor'), may hold values from -0.1875 to 0.1875
- w_out: bfloat16 [1024, 1024], P('tensor'), may hold values from -0.1875 to 0.1875
- norm2_gain: float32 [1024], replicated, may hold values from 0.1 to 1.9
- w_point1: bfloat16 [2, 1024, 1024], P(None, None, 'tensor'), may hold values from -0.1875 to 0.1875
- w_depth: float32 [31, 1024], P(None, 'tensor'), may hold values from -1.5 to 1.5
- bn_scale: float32 [1024], P('tensor'), may hold values from 0.1 to 1.9
- bn_shift: float32 [1024], P('tensor'), may hold values from -1 to 1
- w_point2: bfloat16 [1024, 1024], P('tensor'), may hold values from -0.1875 to 0.1875
Outputs:
- output: bfloat16 [4096, 1024], P(('groups', 'context', 'tensor')), parts along dimension 0
There are 2 independent parts, one for each index of `groups`. A program takes and returns all parts, laid end to end along the dimension named above; an argument that names none is the same for every part. Nothing has to cross between parts.
Inputs may be any that keep to these rules, and one draw needn't show every extreme that they name: `frame_valid`: the transcript frames form a prefix of the window of at least 1024 frames, followed by at least one padded frame.
All inputs are finite; a program needn't handle non-finite values.
Results may differ from a plain program's by a relative error of at most 0.0095.
Values may be sent and summed in bfloat16 or wider, within the bound.
A program may use at most 64 MiB of HBM per device.

v0:
```python
import math
import jax
import jax.numpy as jnp
from jax import lax
from jax.sharding import PartitionSpec as P

HD = 64
NEG = -1e30


def with_halo(block, sides, width):
    for axis, dim in sides:
        count = lax.axis_size(axis)
        forward = [(i, i + 1) for i in range(count - 1)]
        backward = [(target, source) for source, target in forward]
        low = lax.ppermute(
            lax.slice_in_dim(block, block.shape[dim] - width, None, axis=dim), axis, forward
        )
        high = lax.ppermute(lax.slice_in_dim(block, 0, width, axis=dim), axis, backward)
        block = jnp.concatenate([low, block, high], axis=dim)
    return block


def normalize(rows, gain):
    values = rows.astype(jnp.float32)
    center = jnp.mean(values, axis=-1, keepdims=True)
    spread = jnp.mean(jnp.square(values - center), axis=-1, keepdims=True)
    return ((values - center) * lax.rsqrt(spread + 1e-05) * gain).astype(jnp.bfloat16)


def local(
    inputs,
    frame_valid,
    norm1_gain,
    w_query,
    w_key,
    w_value,
    w_out,
    norm2_gain,
    w_point1,
    w_depth,
    bn_scale,
    bn_shift,
    w_point2,
):
    frames = inputs.shape[0]
    local_cols = w_query.shape[1]
    head_dim = HD
    heads_here = local_cols // head_dim
    scale = 1.0 / math.sqrt(head_dim)
    normed = normalize(inputs, norm1_gain)
    query = jnp.dot(normed, w_query, preferred_element_type=jnp.float32).astype(jnp.bfloat16)
    query = query.reshape(frames, heads_here, head_dim)
    keys = jnp.dot(normed, w_key, preferred_element_type=jnp.float32).astype(jnp.bfloat16)
    vals = jnp.dot(normed, w_value, preferred_element_type=jnp.float32).astype(jnp.bfloat16)

    def update(carry, key_blk, val_blk, valid_blk):
        run_max, run_sum, accum = carry
        rows = key_blk.shape[0]
        key_heads = key_blk.reshape(rows, heads_here, head_dim)
        val_heads = val_blk.reshape(rows, heads_here, head_dim)
        scores = (
            jnp.einsum("qhd,khd->hqk", query, key_heads, preferred_element_type=jnp.float32) * scale
        )
        live = (valid_blk > 0)[None, None, :]
        scores = jnp.where(live, scores, NEG)
        new_max = jnp.maximum(run_max, jnp.max(scores, axis=-1))
        weights = jnp.where(live, jnp.exp(scores - new_max[:, :, None]), 0.0)
        factor = jnp.exp(run_max - new_max)
        run_sum = run_sum * factor + jnp.sum(weights, axis=-1)
        mixed = jnp.einsum(
            "hqk,khd->qhd",
            weights.astype(jnp.bfloat16),
            val_heads,
            preferred_element_type=jnp.float32,
        )
        accum = accum * jnp.repeat(factor.T, head_dim, axis=1) + mixed.reshape(frames, local_cols)
        return (new_max, run_sum, accum)

    def visit(carry, key_blk, val_blk, valid_blk):
        return update(carry, key_blk, val_blk, valid_blk)

    start_state = (
        jnp.full((heads_here, frames), NEG, jnp.float32),
        jnp.zeros((heads_here, frames), jnp.float32),
        jnp.zeros((frames, local_cols), jnp.float32),
    )
    carry = start_state
    key_part = lax.all_gather(keys, "context", axis=0, tiled=True)
    val_part = lax.all_gather(vals, "context", axis=0, tiled=True)
    valid_part = lax.all_gather(frame_valid, "context", axis=0, tiled=True)
    rows = key_part.shape[0]
    shards = max(rows // frames, 1)
    group = math.gcd(shards, max(1536 // frames, 1))
    blocks = shards // group
    block_rows = rows // blocks

    def advance(state, items):
        return (visit(state, items[0], items[1], items[2]), None)

    stacked = (
        key_part.reshape(blocks, block_rows, local_cols),
        val_part.reshape(blocks, block_rows, local_cols),
        valid_part.reshape(blocks, block_rows),
    )
    carry, unused = lax.scan(advance, carry, stacked)
    run_max, run_sum, accum = carry
    attended = (accum / jnp.repeat(run_sum.T, head_dim, axis=1)).astype(jnp.bfloat16)
    share = frames // lax.axis_size("tensor")
    first_row = lax.axis_index("tensor") * share
    total = lax.psum(jnp.dot(attended, w_out, preferred_element_type=jnp.float32), "tensor")
    residual = (inputs.astype(jnp.float32) + total).astype(jnp.bfloat16)
    normed_two = normalize(residual, norm2_gain)
    residual_rows = lax.dynamic_slice_in_dim(residual, first_row, share, 0)
    value_half = jnp.dot(normed_two, w_point1[0], preferred_element_type=jnp.float32)
    gate_half = jnp.dot(normed_two, w_point1[1], preferred_element_type=jnp.float32)
    gated = jnp.where(
        (frame_valid > 0)[:, None], value_half * jax.nn.sigmoid(gate_half), 0.0
    ).astype(jnp.bfloat16)
    taps = w_depth.shape[0]
    half = (taps - 1) // 2
    padded = with_halo(gated, (("context", 0),), half)
    depth = jnp.zeros((frames, gated.shape[1]), jnp.float32)
    for tap in range(taps):
        depth = depth + padded[tap : tap + frames].astype(jnp.float32) * w_depth[tap]
    activated = jax.nn.silu(depth * bn_scale + bn_shift).astype(jnp.bfloat16)
    conv_rows = lax.psum_scatter(
        jnp.dot(activated, w_point2, preferred_element_type=jnp.float32).astype(jnp.bfloat16),
        "tensor",
        scatter_dimension=0,
        tiled=True,
    ).astype(jnp.float32)
    return (residual_rows.astype(jnp.float32) + conv_rows).astype(jnp.bfloat16)


def solution(mesh):
    placed = (
        P(("groups", "context"), None),
        P(("groups", "context")),
        P(),
        P(None, "tensor"),
        P(None, "tensor"),
        P(None, "tensor"),
        P("tensor", None),
        P(),
        P(None, None, "tensor"),
        P(None, "tensor"),
        P("tensor"),
        P("tensor"),
        P("tensor", None),
    )
    return jax.shard_map(
        local,
        mesh=mesh,
        in_specs=placed,
        out_specs=P(("groups", "context", "tensor"), None),
        check_vma=False,
    )
```

profile of v0, /device:TPU:0, one launch (start us, length us, event | category | flops | bytes accessed | tf_op | source)
XLA Modules:
  0.0 218.2 jit_solution(7202695658550756041)
XLA Ops:
  12.5 13.7 %all-gather = s32[4,1,512]{2,1,0:T(1,128)S(1)} all-gather(s32[1,1,512]{2,1,0:T(1,128)S(1)} %bitcast.111), channel_id=1, replica_groups=mesh['groups'=2,'context'=4,'tensor'=4] {'context'}, dimensions={0}, use_global_device_ids=true | all-gather | bytes 10240 | tf_op jit(solution)/shard_map/all_gather | solution.py:91
  26.2 1.7 convolution_convert_fusion.2
  27.9 14.0 %all-gather.4.cloned.1.call-done = bf16[2048,256]{1,0:T(8,128)(2,1)} async-done(((bf16[512,256]{1,0:T(8,128)(2,1)}), bf16[2048,256]{1,0:T(8,128)(2,1)}) %all-gather.4.cloned.1.call-update) | async-done | bytes 1048592 | tf_op jit(solution)/shard_map/all_gather | solution.py:89
  41.9 29.0 %all-gather.6.cloned.1.call-done = bf16[2048,256]{1,0:T(8,128)(2,1)} async-done(((bf16[512,256]{1,0:T(8,128)(2,1)}), bf16[2048,256]{1,0:T(8,128)(2,1)}) %all-gather.6.cloned.1.call-update) | async-done | bytes 1048592 | tf_op jit(solution)/shard_map/all_gather | solution.py:90
  70.9 44.4 %while.15 = (s32[]{:T(128)}, f32[4,512]{1,0:T(4,128)S(1)}, f32[4,512]{1,0:T(4,128)S(1)}, f32[512,256]{0,1:T(8,128)S(1)}, s32[4,512]{1,0:T(4,128)S(1)}, /*index=5...) while((s32[]{:T(128)}, f32[4,512]{1,0:T(4,128)S(1)}, ...), condition=%wide.region_5.6_spmd.clone, body=%wide.region_2.5_spmd.clone.sunk | while | flops 282472960 | bytes 17698944 | solution.py:106
  72.2 2.9 %bitcast_reduce_fusion.2 = (f32[4,512]{1,0:T(4,128)S(1)}, f32[4,512,512]{2,1,0:T(8,128)}) fusion(pred[512]{0:T(512)(128)(4,1)S(1)} %compare_reduce_fusion.2, bf16[512,4,64]{0,2,1:T(8,128)(2,1)S(1)} %bitcast.104, bf16[512,4,64]{0,2,1:T(8,128)(2,1)S(1)} %get-tuple-element.237), kind=kOutput, calls=%fused_computation.1.clone.1 | convolution fusion | flops 137361408 | bytes 4727296 | tf_op jit(solution)/shard_map/while/body/eval_jaxpr/qhd,khd->hqk/dot_general | solution.py:63
  75.1 3.3 %fusion.96 = f32[4,512]{1,0:T(4,128)S(1)} fusion(f32[4,512,512]{2,1,0:T(8,128)} %get-tuple-element.208, f32[4,512]{1,0:T(4,128)S(1)} %get-tuple-element.232, pred[512]{0:T(512)(128)(4,1)S(1)} %compare_reduce_fusion.2), kind=kLoop, calls=%fused_computation.6.clone.1 | loop fusion | flops 5240832 | bytes 4211200 | tf_op jit(solution)/shard_map/while/body/eval_jaxpr/reduce_sum | solution.py:70
  78.6 3.3 %fusion.98 = f32[4,64,512]{2,1,0:T(8,128)S(1)} fusion(bf16[512,4,64]{0,2,1:T(8,128)(2,1)S(1)} %bitcast.106, f32[4,512,512]{2,1,0:T(8,128)} %get-tuple-element.208, f32[4,512]{1,0:T(4,128)S(1)} %get-tuple-element.232, pred[512]{0:T(512)(128)(4,1)S(1)} %compare_reduce_fusion.2), kind=kOutput, calls=%fused_computation.7.clone.1 | convolution fusion | flops 139460608 | bytes 4989440 | tf_op jit(solution)/shard_map/while/body/eval_jaxpr/hqk,khd->qhd/dot_general | solution.py:71
  83.3 2.9 %bitcast_reduce_fusion.2 = (f32[4,512]{1,0:T(4,128)S(1)}, f32[4,512,512]{2,1,0:T(8,128)}) fusion(pred[512]{0:T(512)(128)(4,1)S(1)} %compare_reduce_fusion.2, bf16[512,4,64]{0,2,1:T(8,128)(2,1)S(1)} %bitcast.104, bf16[512,4,64]{0,2,1:T(8,128)(2,1)S(1)} %get-tuple-element.237), kind=kOutput, calls=%fused_computation.1.clone.1 | convolution fusion | flops 137361408 | bytes 4727296 | tf_op jit(solution)/shard_map/while/body/eval_jaxpr/qhd,khd->hqk/dot_general | solution.py:63
  86.2 3.3 %fusion.96 = f32[4,512]{1,0:T(4,128)S(1)} fusion(f32[4,512,512]{2,1,0:T(8,128)} %get-tuple-element.208, f32[4,512]{1,0:T(4,128)S(1)} %get-tuple-element.232, pred[512]{0:T(512)(128)(4,1)S(1)} %compare_reduce_fusion.2), kind=kLoop, calls=%fused_computation.6.clone.1 | loop fusion | flops 5240832 | bytes 4211200 | tf_op jit(solution)/shard_map/while/body/eval_jaxpr/reduce_sum | solution.py:70
  89.7 3.3 %fusion.98 = f32[4,64,512]{2,1,0:T(8,128)S(1)} fusion(bf16[512,4,64]{0,2,1:T(8,128)(2,1)S(1)} %bitcast.106, f32[4,512,512]{2,1,0:T(8,128)} %get-tuple-element.208, f32[4,512]{1,0:T(4,128)S(1)} %get-tuple-element.232, pred[512]{0:T(512)(128)(4,1)S(1)} %compare_reduce_fusion.2), kind=kOutput, calls=%fused_computation.7.clone.1 | convolution fusion | flops 139460608 | bytes 4989440 | tf_op jit(solution)/shard_map/while/body/eval_jaxpr/hqk,khd->qhd/dot_general | solution.py:71
  94.4 2.9 %bitcast_reduce_fusion.2 = (f32[4,512]{1,0:T(4,128)S(1)}, f32[4,512,512]{2,1,0:T(8,128)}) fusion(pred[512]{0:T(512)(128)(4,1)S(1)} %compare_reduce_fusion.2, bf16[512,4,64]{0,2,1:T(8,128)(2,1)S(1)} %bitcast.104, bf16[512,4,64]{0,2,1:T(8,128)(2,1)S(1)} %get-tuple-element.237), kind=kOutput, calls=%fused_computation.1.clone.1 | convolution fusion | flops 137361408 | bytes 4727296 | tf_op jit(solution)/shard_map/while/body/eval_jaxpr/qhd,khd->hqk/dot_general | solution.py:63
  97.3 3.3 %fusion.96 = f32[4,512]{1,0:T(4,128)S(1)} fusion(f32[4,512,512]{2,1,0:T(8,128)} %get-tuple-element.208, f32[4,512]{1,0:T(4,128)S(1)} %get-tuple-element.232, pred[512]{0:T(512)(128)(4,1)S(1)} %compare_reduce_fusion.2), kind=kLoop, calls=%fused_computation.6.clone.1 | loop fusion | flops 5240832 | bytes 4211200 | tf_op jit(solution)/shard_map/while/body/eval_jaxpr/reduce_sum | solution.py:70
  100.8 3.3 %fusion.98 = f32[4,64,512]{2,1,0:T(8,128)S(1)} fusion(bf16[512,4,64]{0,2,1:T(8,128)(2,1)S(1)} %bitcast.106, f32[4,512,512]{2,1,0:T(8,128)} %get-tuple-element.208, f32[4,512]{1,0:T(4,128)S(1)} %get-tuple-element.232, pred[512]{0:T(512)(128)(4,1)S(1)} %compare_reduce_fusion.2), kind=kOutput, calls=%fused_computation.7.clone.1 | convolution fusion | flops 139460608 | bytes 4989440 | tf_op jit(solution)/shard_map/while/body/eval_jaxpr/hqk,khd->qhd/dot_general | solution.py:71
  105.5 2.9 %bitcast_reduce_fusion.2 = (f32[4,512]{1,0:T(4,128)S(1)}, f32[4,512,512]{2,1,0:T(8,128)}) fusion(pred[512]{0:T(512)(128)(4,1)S(1)} %compare_reduce_fusion.2, bf16[512,4,64]{0,2,1:T(8,128)(2,1)S(1)} %bitcast.104, bf16[512,4,64]{0,2,1:T(8,128)(2,1)S(1)} %get-tuple-element.237), kind=kOutput, calls=%fused_computation.1.clone.1 | convolution fusion | flops 137361408 | bytes 4727296 | tf_op jit(solution)/shard_map/while/body/eval_jaxpr/qhd,khd->hqk/dot_general | solution.py:63
  108.4 3.3 %fusion.96 = f32[4,512]{1,0:T(4,128)S(1)} fusion(f32[4,512,512]{2,1,0:T(8,128)} %get-tuple-element.208, f32[4,512]{1,0:T(4,128)S(1)} %get-tuple-element.232, pred[512]{0:T(512)(128)(4,1)S(1)} %compare_reduce_fusion.2), kind=kLoop, calls=%fused_computation.6.clone.1 | loop fusion | flops 5240832 | bytes 4211200 | tf_op jit(solution)/shard_map/while/body/eval_jaxpr/reduce_sum | solution.py:70
  111.9 3.3 %fusion.98 = f32[4,64,512]{2,1,0:T(8,128)S(1)} fusion(bf16[512,4,64]{0,2,1:T(8,128)(2,1)S(1)} %bitcast.106, f32[4,512,512]{2,1,0:T(8,128)} %get-tuple-element.208, f32[4,512]{1,0:T(4,128)S(1)} %get-tuple-element.232, pred[512]{0:T(512)(128)(4,1)S(1)} %compare_reduce_fusion.2), kind=kOutput, calls=%fused_computation.7.clone.1 | convolution fusion | flops 139460608 | bytes 4989440 | tf_op jit(solution)/shard_map/while/body/eval_jaxpr/hqk,khd->qhd/dot_general | solution.py:71
  115.4 1.8 fusion.73
  117.4 50.9 %all-reduce.2.cloned.1.call-done = f32[512,1024]{1,0:T(8,128)} async-done(((f32[512,1024]{1,0:T(8,128)}), f32[512,1024]{1,0:T(8,128)}) %all-reduce.2.cloned.1.call-update) | async-done | bytes 2097168 | tf_op jit(solution)/shard_map/psum | solution.py:111
  168.3 2.0 convert_reduce_fusion.1
  173.2 4.5 %collective-permute-start = (bf16[15,256]{1,0:T(8,128)(2,1)S(1)}, bf16[15,256]{1,0:T(8,128)(2,1)S(1)}, u32[]{:S(2)}, u32[]{:S(2)}) collective-permute-start(bf16[15,256]{1,0:T(8,128)(2,1)S(1)} %get-tuple-element.117), channel_id=1, source_target_pairs={{0,4},{4,8},{8,12},{1,5},{5,9},{9,13},{2,6},{6,10},{10,14},{3,7},{... | collective-permute-start | bytes 23048 | tf_op jit(solution)/shard_map/ppermute | solution.py:16
  179.1 4.9 %convolution_convert_fusion = bf16[512,1024]{1,0:T(8,128)(2,1)} fusion(bf16[256,1024]{1,0:T(8,128)(2,1)S(1)} %copy-done.7, bf16[512,256]{1,0:T(8,128)(2,1)S(1)} %fusion.28, bf16[15,256]{1,0:T(8,128)(2,1)S(1)} %collective-permute-done.1, bf16[15,256]{1,0:T(8,128)(2,1)S(1)} %collective-permute-done, f32[256]{0:T(256)S(1)} %copy-done.10, ...), kind=kOutput, calls=%fused_computation.67 | convolution fusion | flops 293732352 | bytes 1884160 | tf_op jit(solution)/shard_map/dot_general | solution.py:128
  184.0 26.0 %reduce-scatter.2.cloned.1.call-done = bf16[128,1024]{1,0:T(8,128)(2,1)} async-done(((bf16[512,1024]{1,0:T(8,128)(2,1)}), bf16[128,1024]{1,0:T(8,128)(2,1)}) %reduce-scatter.2.cloned.1.call-update) | async-done | bytes 262160 | tf_op jit(solution)/shard_map/reduce_scatter | solution.py:127
  209.9 1.7 add_convert_fusion
  (87 shorter events, 16.5 us)
Async XLA Ops:
  6.5 108.9 %copy-start = (bf16[256,1024]{1,0:T(8,128)(2,1)S(1)}, bf16[256,1024]{1,0:T(8,128)(2,1)}, u32[]{:S(2)}) copy-start(bf16[256,1024]{1,0:T(8,128)(2,1)} %param.21) | copy-start | bytes 1572868
  6.5 3.3 %copy-start.1 = (bf16[512,1024]{1,0:T(8,128)(2,1)S(1)}, bf16[512,1024]{1,0:T(8,128)(2,1)}, u32[]{:S(2)}) copy-start(bf16[512,1024]{1,0:T(8,128)(2,1)} %param.15) | copy-start | bytes 3145732
  6.5 3.3 %copy-start.5 = (bf16[1024,256]{1,0:T(8,128)(2,1)S(1)}, bf16[1024,256]{1,0:T(8,128)(2,1)}, u32[]{:S(2)}) copy-start(bf16[1024,256]{1,0:T(8,128)(2,1)} %param.19) | copy-start | bytes 1572868
  6.5 3.3 %copy-start.8 = (f32[1024]{0:T(1024)S(1)}, f32[1024]{0:T(1024)}, u32[]{:S(2)}) copy-start(f32[1024]{0:T(1024)} %param.17) | copy-start | bytes 12292
  6.5 35.4 %all-gather.4.cloned.1.call-start = ((), (), s32[]{:S(2)}) async-start(), calls=%async_computation.1 | async-start | bytes 1310720 | tf_op jit(solution)/shard_map/all_gather | solution.py:89
  9.8 1.4 copy-start.6
  11.1 1.4 copy-start.3
  11.1 59.8 %all-gather.6.cloned.1.call-start = ((), (), s32[]{:S(2)}) async-start(), calls=%async_computation.2 | async-start | bytes 1310720 | tf_op jit(solution)/shard_map/all_gather | solution.py:90
  12.4 155.9 %all-reduce.2.cloned.1.call-start = ((), (), s32[]{:S(2)}) async-start(), calls=%async_computation.3 | async-start | bytes 4194304 | tf_op jit(solution)/shard_map/psum | solution.py:111
  115.4 1.9 copy-start.2
  117.2 92.7 %reduce-scatter.2.cloned.1.call-start = ((), (), s32[]{:S(2)}) async-start(), calls=%async_computation.4 | async-start | bytes 1310720 | tf_op jit(solution)/shard_map/reduce_scatter | solution.py:127
  117.3 53.4 %copy-start.9 = (f32[1024]{0:T(1024)S(1)}, f32[1024]{0:T(1024)}, u32[]{:S(2)}) copy-start(f32[1024]{0:T(1024)} %param.22) | copy-start | bytes 12292
  168.3 2.4 %copy-start.4 = (bf16[2,1024,256]{2,1,0:T(8,128)(2,1)S(1)}, bf16[2,1024,256]{2,1,0:T(8,128)(2,1)}, u32[]{:S(2)}) copy-start(bf16[2,1024,256]{2,1,0:T(8,128)(2,1)} %param.23) | copy-start | bytes 3145732
  171.3 7.8 %copy-start.7 = (bf16[256,1024]{1,0:T(8,128)(2,1)S(1)}, bf16[256,1024]{1,0:T(8,128)(2,1)}, u32[]{:S(2)}) copy-start(bf16[256,1024]{1,0:T(8,128)(2,1)} %param.27) | copy-start | bytes 1572868
  171.3 7.8 %copy-start.10 = (f32[256]{0:T(256)S(1)}, f32[256]{0:T(256)}, u32[]{:S(2)}) copy-start(f32[256]{0:T(256)} %param.26) | copy-start | bytes 3076
  171.3 7.8 %copy-start.11 = (f32[256]{0:T(256)S(1)}, f32[256]{0:T(256)}, u32[]{:S(2)}) copy-start(f32[256]{0:T(256)} %param.25) | copy-start | bytes 3076
  171.9 5.9 %collective-permute-start.1 = (bf16[15,256]{1,0:T(8,128)(2,1)S(1)}, bf16[15,256]{1,0:T(8,128)(2,1)S(1)}, u32[]{:S(2)}, u32[]{:S(2)}) collective-permute-start(bf16[15,256]{1,0:T(8,128)(2,1)S(1)} %get-tuple-element.118), channel_id=1, source_target_pairs={{4,0},{8,4},{12,8},{5,1},{9,5},{13,9},{6,2},{10,6},{14,10},{7,3},{... | collective-permute-start | bytes 23048 | tf_op jit(solution)/shard_map/ppermute | solution.py:19
  173.2 5.9 %collective-permute-start = (bf16[15,256]{1,0:T(8,128)(2,1)S(1)}, bf16[15,256]{1,0:T(8,128)(2,1)S(1)}, u32[]{:S(2)}, u32[]{:S(2)}) collective-permute-start(bf16[15,256]{1,0:T(8,128)(2,1)S(1)} %get-tuple-element.117), channel_id=1, source_target_pairs={{0,4},{4,8},{8,12},{1,5},{5,9},{9,13},{2,6},{6,10},{10,14},{3,7},{... | collective-permute-start | bytes 23048 | tf_op jit(solution)/shard_map/ppermute | solution.py:16
Sparse Core Ops, SparseCore 0:
  11.2 30.6 all-gather.3
  43.5 27.3 all-gather.5
  117.4 50.8 all-reduce.1
  184.1 25.8 reduce-scatter.1
where the time goes:
time: 219 us; the launch traced here: 218 us
  waiting for transfers between devices  121 us (55%)
  matrix products  36.7 us (17%)
  other arithmetic  21.4 us (10%)
  blocking collectives  13.7 us (6%)
  between operations  13.4 us (6%)
  starting transfers between devices  6 us (3%)
  local copies, waits for them, and re-layouts  5.5 us (3%)
    psum x1, waiting for transfers between devices, local(): lax.psum(jnp.dot(attended, w_out, preferred_element_type=jnp.float32), 't...  50.9 us
    all_gather x1, waiting for transfers between devices, local(): val_part = lax.all_gather(vals, 'context', axis=0, tiled=True)  29 us
    reduce_scatter x1, waiting for transfers between devices, local(): lax.psum_scatter(jnp.dot(activated, w_point2, preferred_element_type=jnp....  26 us
    all_gather x1, waiting for transfers between devices, local(): key_part = lax.all_gather(keys, 'context', axis=0, tiled=True)  14 us
    all_gather x1, blocking collectives, local(): valid_part = lax.all_gather(frame_valid, 'context', axis=0, tiled=True)  13.7 us
    dot_general x4, matrix products, update(): jnp.einsum('hqk,khd->qhd', weights.astype(jnp.bfloat16), val_heads, prefe...  13.1 us
    reduce_sum x4, other arithmetic, update(): run_sum = run_sum * factor + jnp.sum(weights, axis=-1)  13.1 us
    dot_general x4, matrix products, update(): jnp.einsum('qhd,khd->hqk', query, key_heads, preferred_element_type=jnp.f...  11.6 us
  transfers between devices with their start and end apart: 6, of which 5 were waited for; matrix products, arithmetic and copies ran while one was open for 1% of the time, Pallas kernels for 0%

commit v1 on v0

--- a/solution.py
+++ b/solution.py
@@ -86,7 +86,14 @@
         jnp.zeros((frames, local_cols), jnp.float32),
     )
     carry = start_state
-    key_part = lax.all_gather(keys, "context", axis=0, tiled=True)
+    ring = [keys]
+    for hop in range(3):
+        ring.append(lax.ppermute(ring[-1], "context", [(dev, (dev + 1) % 4) for dev in range(4)]))
+    key_part = jnp.roll(
+        jnp.concatenate(ring[::-1], axis=0),
+        (lax.axis_index("context") + 1) * ring[0].shape[0],
+        axis=0,
+    )
     val_part = lax.all_gather(vals, "context", axis=0, tiled=True)
     valid_part = lax.all_gather(frame_valid, "context", axis=0, tiled=True)
     rows = key_part.shape[0]

time: 219 us -> 206 us (0.941)
  waiting for transfers between devices: 121 us -> 105 us
  starting transfers between devices: 6 us -> 9.09 us
    all_gather x1, waiting for transfers between devices: 29 us -> 4.59 us  [local(): val_part = lax.all_gather(vals, 'context', axis=0, tiled=True)]
    ppermute x0 -> x3, waiting for transfers between devices: none -> 21.8 us  [local(): lax.ppermute(ring[-1], 'context', [(dev, (dev + 1) % 4) for dev in range(...]
    all_gather x1 -> x0, waiting for transfers between devices: 14 us -> none  [local(): key_part = lax.all_gather(keys, 'context', axis=0, tiled=True)]
    ppermute x0 -> x3, starting transfers between devices: none -> 3.14 us  [local(): lax.ppermute(ring[-1], 'context', [(dev, (dev + 1) % 4) for dev in range(...]
  transfers between devices with their start and end apart: 6 -> 8, of which waited for: 5 -> 6; matrix products, arithmetic and copies ran while one was open for 1% -> 2% of each run, Pallas kernels for 0% -> 0%
where the time goes in v1:
time: 206 us
  waiting for transfers between devices  105 us (51%)
  matrix products  36 us (17%)
  other arithmetic  21.5 us (10%)
  blocking collectives  13.9 us (7%)
  between operations  13.4 us (7%)
  starting transfers between devices  9.09 us (4%)
  local copies, waits for them, and re-layouts  6.74 us (3%)
    psum x1, waiting for transfers between devices, local(): lax.psum(jnp.dot(attended, w_out, preferred_element_type=jnp.float32), 't...  50.9 us
    reduce_scatter x1, waiting for transfers between devices, local(): lax.psum_scatter(jnp.dot(activated, w_point2, preferred_element_type=jnp....  26 us
    ppermute x3, waiting for transfers between devices, local(): lax.ppermute(ring[-1], 'context', [(dev, (dev + 1) % 4) for dev in range(...  21.8 us
    all_gather x1, blocking collectives, local(): valid_part = lax.all_gather(frame_valid, 'context', axis=0, tiled=True)  13.9 us
    dot_general x4, matrix products, update(): jnp.einsum('hqk,khd->qhd', weights.astype(jnp.bfloat16), val_heads, prefe...  13.1 us
    reduce_sum x4, other arithmetic, update(): run_sum = run_sum * factor + jnp.sum(weights, axis=-1)  13.1 us
    dot_general x4, matrix products, update(): jnp.einsum('qhd,khd->hqk', query, key_heads, preferred_element_type=jnp.f...  11.6 us
    dynamic_slice x12, local copies, waits for them, and re-layouts, local(): carry, unused = lax.scan(advance, carry, stacked)  5.39 us
  transfers between devices with their start and end apart: 8, of which 6 were waited for; matrix products, arithmetic and copies ran while one was open for 2% of the time, Pallas kernels for 0%

profile of v1, /device:TPU:0, one launch (start us, length us, event | category | flops | bytes accessed | tf_op | source)
XLA Modules:
  0.0 205.5 jit_solution(6507195544647511607)
XLA Ops:
  10.4 3.1 %collective-permute-start = (bf16[512,256]{1,0:T(8,128)(2,1)S(1)}, bf16[512,256]{1,0:T(8,128)(2,1)S(1)}, u32[]{:S(2)}, u32[]{:S(2)}) collective-permute-start(bf16[512,256]{1,0:T(8,128)(2,1)S(1)} %convolution_convert_fusion.3), channel_id=1, source_target_pairs={{0,4},{4,8},{8,12},{12,0},{1,5},{5,9},{9,13},{13,1},{2,6},{6,10},{... | collective-permute-start | bytes 786440 | tf_op jit(solution)/shard_map/ppermute | solution.py:91
  13.5 8.3 %collective-permute-done = bf16[512,256]{1,0:T(8,128)(2,1)S(1)} collective-permute-done((bf16[512,256]{1,0:T(8,128)(2,1)S(1)}, bf16[512,256]{1,0:T(8,128)(2,1)S(1)}, u32[]{:S(2)}, u32[]{:S(2)}) %collective-permute-start) | collective-permute-done | bytes 262176 | tf_op jit(solution)/shard_map/ppermute | solution.py:91
  23.2 13.9 %all-gather = s32[4,1,512]{2,1,0:T(1,128)S(1)} all-gather(s32[1,1,512]{2,1,0:T(1,128)S(1)} %bitcast.111), channel_id=1, replica_groups=mesh['groups'=2,'context'=4,'tensor'=4] {'context'}, dimensions={0}, use_global_device_ids=true | all-gather | bytes 10240 | tf_op jit(solution)/shard_map/all_gather | solution.py:98
  39.0 13.4 %collective-permute-done.2 = bf16[512,256]{1,0:T(8,128)(2,1)S(1)} collective-permute-done((bf16[512,256]{1,0:T(8,128)(2,1)S(1)}, bf16[512,256]{1,0:T(8,128)(2,1)S(1)}, u32[]{:S(2)}, u32[]{:S(2)}) %collective-permute-start.2) | collective-permute-done | bytes 262176 | tf_op jit(solution)/shard_map/ppermute | solution.py:91
  53.7 4.6 %all-gather.3.cloned.1.call-done = bf16[2048,256]{1,0:T(8,128)(2,1)} async-done(((bf16[512,256]{1,0:T(8,128)(2,1)}), bf16[2048,256]{1,0:T(8,128)(2,1)}) %all-gather.3.cloned.1.call-update) | async-done | bytes 1048592 | tf_op jit(solution)/shard_map/all_gather | solution.py:97
  58.3 44.4 %while.15 = (s32[]{:T(128)}, f32[4,512]{1,0:T(4,128)S(1)}, f32[4,512]{1,0:T(4,128)S(1)}, f32[512,256]{0,1:T(8,128)S(1)}, s32[4,512]{1,0:T(4,128)S(1)}, /*index=5...) while((s32[]{:T(128)}, f32[4,512]{1,0:T(4,128)S(1)}, ...), condition=%wide.region_5.6_spmd.clone, body=%wide.region_2.5_spmd.clone.sunk | while | flops 282472960 | bytes 17698944 | solution.py:113
  59.5 2.9 %bitcast_reduce_fusion.2 = (f32[4,512]{1,0:T(4,128)S(1)}, f32[4,512,512]{2,1,0:T(8,128)}) fusion(pred[512]{0:T(512)(128)(4,1)S(1)} %compare_reduce_fusion.2, bf16[512,4,64]{0,2,1:T(8,128)(2,1)S(1)} %bitcast.104, bf16[512,4,64]{0,2,1:T(8,128)(2,1)S(1)} %get-tuple-element.245), kind=kOutput, calls=%fused_computation.1.clone.1 | convolution fusion | flops 137361408 | bytes 4727296 | tf_op jit(solution)/shard_map/while/body/eval_jaxpr/qhd,khd->hqk/dot_general | solution.py:63
  62.5 3.3 %fusion.96 = f32[4,512]{1,0:T(4,128)S(1)} fusion(f32[4,512,512]{2,1,0:T(8,128)} %get-tuple-element.216, f32[4,512]{1,0:T(4,128)S(1)} %get-tuple-element.240, pred[512]{0:T(512)(128)(4,1)S(1)} %compare_reduce_fusion.2), kind=kLoop, calls=%fused_computation.6.clone.1 | loop fusion | flops 5240832 | bytes 4211200 | tf_op jit(solution)/shard_map/while/body/eval_jaxpr/reduce_sum | solution.py:70
  65.9 3.3 %fusion.98 = f32[4,64,512]{2,1,0:T(8,128)S(1)} fusion(bf16[512,4,64]{0,2,1:T(8,128)(2,1)S(1)} %bitcast.106, f32[4,512,512]{2,1,0:T(8,128)} %get-tuple-element.216, f32[4,512]{1,0:T(4,128)S(1)} %get-tuple-element.240, pred[512]{0:T(512)(128)(4,1)S(1)} %compare_reduce_fusion.2), kind=kOutput, calls=%fused_computation.7.clone.1 | convolution fusion | flops 139460608 | bytes 4989440 | tf_op jit(solution)/shard_map/while/body/eval_jaxpr/hqk,khd->qhd/dot_general | solution.py:71
  70.6 2.9 %bitcast_reduce_fusion.2 = (f32[4,512]{1,0:T(4,128)S(1)}, f32[4,512,512]{2,1,0:T(8,128)}) fusion(pred[512]{0:T(512)(128)(4,1)S(1)} %compare_reduce_fusion.2, bf16[512,4,64]{0,2,1:T(8,128)(2,1)S(1)} %bitcast.104, bf16[512,4,64]{0,2,1:T(8,128)(2,1)S(1)} %get-tuple-element.245), kind=kOutput, calls=%fused_computation.1.clone.1 | convolution fusion | flops 137361408 | bytes 4727296 | tf_op jit(solution)/shard_map/while/body/eval_jaxpr/qhd,khd->hqk/dot_general | solution.py:63
  73.6 3.3 %fusion.96 = f32[4,512]{1,0:T(4,128)S(1)} fusion(f32[4,512,512]{2,1,0:T(8,128)} %get-tuple-element.216, f32[4,512]{1,0:T(4,128)S(1)} %get-tuple-element.240, pred[512]{0:T(512)(128)(4,1)S(1)} %compare_reduce_fusion.2), kind=kLoop, calls=%fused_computation.6.clone.1 | loop fusion | flops 5240832 | bytes 4211200 | tf_op jit(solution)/shard_map/while/body/eval_jaxpr/reduce_sum | solution.py:70
  77.0 3.3 %fusion.98 = f32[4,64,512]{2,1,0:T(8,128)S(1)} fusion(bf16[512,4,64]{0,2,1:T(8,128)(2,1)S(1)} %bitcast.106, f32[4,512,512]{2,1,0:T(8,128)} %get-tuple-element.216, f32[4,512]{1,0:T(4,128)S(1)} %get-tuple-element.240, pred[512]{0:T(512)(128)(4,1)S(1)} %compare_reduce_fusion.2), kind=kOutput, calls=%fused_computation.7.clone.1 | convolution fusion | flops 139460608 | bytes 4989440 | tf_op jit(solution)/shard_map/while/body/eval_jaxpr/hqk,khd->qhd/dot_general | solution.py:71
  81.7 2.9 %bitcast_reduce_fusion.2 = (f32[4,512]{1,0:T(4,128)S(1)}, f32[4,512,512]{2,1,0:T(8,128)}) fusion(pred[512]{0:T(512)(128)(4,1)S(1)} %compare_reduce_fusion.2, bf16[512,4,64]{0,2,1:T(8,128)(2,1)S(1)} %bitcast.104, bf16[512,4,64]{0,2,1:T(8,128)(2,1)S(1)} %get-tuple-element.245), kind=kOutput, calls=%fused_computation.1.clone.1 | convolution fusion | flops 137361408 | bytes 4727296 | tf_op jit(solution)/shard_map/while/body/eval_jaxpr/qhd,khd->hqk/dot_general | solution.py:63
  84.7 3.3 %fusion.96 = f32[4,512]{1,0:T(4,128)S(1)} fusion(f32[4,512,512]{2,1,0:T(8,128)} %get-tuple-element.216, f32[4,512]{1,0:T(4,128)S(1)} %get-tuple-element.240, pred[512]{0:T(512)(128)(4,1)S(1)} %compare_reduce_fusion.2), kind=kLoop, calls=%fused_computation.6.clone.1 | loop fusion | flops 5240832 | bytes 4211200 | tf_op jit(solution)/shard_map/while/body/eval_jaxpr/reduce_sum | solution.py:70
  88.1 3.3 %fusion.98 = f32[4,64,512]{2,1,0:T(8,128)S(1)} fusion(bf16[512,4,64]{0,2,1:T(8,128)(2,1)S(1)} %bitcast.106, f32[4,512,512]{2,1,0:T(8,128)} %get-tuple-element.216, f32[4,512]{1,0:T(4,128)S(1)} %get-tuple-element.240, pred[512]{0:T(512)(128)(4,1)S(1)} %compare_reduce_fusion.2), kind=kOutput, calls=%fused_computation.7.clone.1 | convolution fusion | flops 139460608 | bytes 4989440 | tf_op jit(solution)/shard_map/while/body/eval_jaxpr/hqk,khd->qhd/dot_general | solution.py:71
  92.8 2.9 %bitcast_reduce_fusion.2 = (f32[4,512]{1,0:T(4,128)S(1)}, f32[4,512,512]{2,1,0:T(8,128)}) fusion(pred[512]{0:T(512)(128)(4,1)S(1)} %compare_reduce_fusion.2, bf16[512,4,64]{0,2,1:T(8,128)(2,1)S(1)} %bitcast.104, bf16[512,4,64]{0,2,1:T(8,128)(2,1)S(1)} %get-tuple-element.245), kind=kOutput, calls=%fused_computation.1.clone.1 | convolution fusion | flops 137361408 | bytes 4727296 | tf_op jit(solution)/shard_map/while/body/eval_jaxpr/qhd,khd->hqk/dot_general | solution.py:63
  95.8 3.3 %fusion.96 = f32[4,512]{1,0:T(4,128)S(1)} fusion(f32[4,512,512]{2,1,0:T(8,128)} %get-tuple-element.216, f32[4,512]{1,0:T(4,128)S(1)} %get-tuple-element.240, pred[512]{0:T(512)(128)(4,1)S(1)} %compare_reduce_fusion.2), kind=kLoop, calls=%fused_computation.6.clone.1 | loop fusion | flops 5240832 | bytes 4211200 | tf_op jit(solution)/shard_map/while/body/eval_jaxpr/reduce_sum | solution.py:70
  99.2 3.3 %fusion.98 = f32[4,64,512]{2,1,0:T(8,128)S(1)} fusion(bf16[512,4,64]{0,2,1:T(8,128)(2,1)S(1)} %bitcast.106, f32[4,512,512]{2,1,0:T(8,128)} %get-tuple-element.216, f32[4,512]{1,0:T(4,128)S(1)} %get-tuple-element.240, pred[512]{0:T(512)(128)(4,1)S(1)} %compare_reduce_fusion.2), kind=kOutput, calls=%fused_computation.7.clone.1 | convolution fusion | flops 139460608 | bytes 4989440 | tf_op jit(solution)/shard_map/while/body/eval_jaxpr/hqk,khd->qhd/dot_general | solution.py:71
  102.8 1.8 fusion.73
  104.7 50.9 %all-reduce.2.cloned.1.call-done = f32[512,1024]{1,0:T(8,128)} async-done(((f32[512,1024]{1,0:T(8,128)}), f32[512,1024]{1,0:T(8,128)}) %all-reduce.2.cloned.1.call-update) | async-done | bytes 2097168 | tf_op jit(solution)/shard_map/psum | solution.py:118
  155.6 2.0 convert_reduce_fusion.1
  160.5 4.5 %collective-permute-start.3 = (bf16[15,256]{1,0:T(8,128)(2,1)S(1)}, bf16[15,256]{1,0:T(8,128)(2,1)S(1)}, u32[]{:S(2)}, u32[]{:S(2)}) collective-permute-start(bf16[15,256]{1,0:T(8,128)(2,1)S(1)} %get-tuple-element.125), channel_id=1, source_target_pairs={{0,4},{4,8},{8,12},{1,5},{5,9},{9,13},{2,6},{6,10},{10,14},{3,7},{... | collective-permute-start | bytes 23048 | tf_op jit(solution)/shard_map/ppermute | solution.py:16
  166.4 4.9 %convolution_convert_fusion = bf16[512,1024]{1,0:T(8,128)(2,1)} fusion(bf16[256,1024]{1,0:T(8,128)(2,1)S(1)} %copy-done.7, bf16[512,256]{1,0:T(8,128)(2,1)S(1)} %fusion.28, bf16[15,256]{1,0:T(8,128)(2,1)S(1)} %collective-permute-done.4, bf16[15,256]{1,0:T(8,128)(2,1)S(1)} %collective-permute-done.3, f32[256]{0:T(256)S(1)} %copy-done.10, ...), kind=kOutput, calls=%fused_computation.67 | convolution fusion | flops 293732352 | bytes 1884160 | tf_op jit(solution)/shard_map/dot_general | solution.py:135
  171.3 26.0 %reduce-scatter.2.cloned.1.call-done = bf16[128,1024]{1,0:T(8,128)(2,1)} async-done(((bf16[512,1024]{1,0:T(8,128)(2,1)}), bf16[128,1024]{1,0:T(8,128)(2,1)}) %reduce-scatter.2.cloned.1.call-update) | async-done | bytes 262160 | tf_op jit(solution)/shard_map/reduce_scatter | solution.py:134
  (99 shorter events, 20.6 us)
Async XLA Ops:
  6.5 96.2 %copy-start = (bf16[256,1024]{1,0:T(8,128)(2,1)S(1)}, bf16[256,1024]{1,0:T(8,128)(2,1)}, u32[]{:S(2)}) copy-start(bf16[256,1024]{1,0:T(8,128)(2,1)} %param.21) | copy-start | bytes 1572868
  6.5 3.3 %copy-start.1 = (bf16[512,1024]{1,0:T(8,128)(2,1)S(1)}, bf16[512,1024]{1,0:T(8,128)(2,1)}, u32[]{:S(2)}) copy-start(bf16[512,1024]{1,0:T(8,128)(2,1)} %param.15) | copy-start | bytes 3145732
  6.5 3.4 %copy-start.5 = (bf16[1024,256]{1,0:T(8,128)(2,1)S(1)}, bf16[1024,256]{1,0:T(8,128)(2,1)}, u32[]{:S(2)}) copy-start(bf16[1024,256]{1,0:T(8,128)(2,1)} %param.19) | copy-start | bytes 1572868
  6.5 3.4 %copy-start.8 = (f32[1024]{0:T(1024)S(1)}, f32[1024]{0:T(1024)}, u32[]{:S(2)}) copy-start(f32[1024]{0:T(1024)} %param.17) | copy-start | bytes 12292
  6.5 51.7 %all-gather.3.cloned.1.call-start = ((), (), s32[]{:S(2)}) async-start(), calls=%async_computation.1 | async-start | bytes 1310720 | tf_op jit(solution)/shard_map/all_gather | solution.py:97
  8.2 13.7 %copy-start.6 = (bf16[1024,256]{1,0:T(8,128)(2,1)S(1)}, bf16[1024,256]{1,0:T(8,128)(2,1)}, u32[]{:S(2)}) copy-start(bf16[1024,256]{1,0:T(8,128)(2,1)} %param.20) | copy-start | bytes 1572868
  10.4 12.8 %copy-start.3 = (s32[512]{0:T(512)S(1)}, s32[512]{0:T(512)}, u32[]{:S(2)}) copy-start(s32[512]{0:T(512)} %param.16) | copy-start | bytes 6148
  10.4 11.4 %collective-permute-start = (bf16[512,256]{1,0:T(8,128)(2,1)S(1)}, bf16[512,256]{1,0:T(8,128)(2,1)S(1)}, u32[]{:S(2)}, u32[]{:S(2)}) collective-permute-start(bf16[512,256]{1,0:T(8,128)(2,1)S(1)} %convolution_convert_fusion.3), channel_id=1, source_target_pairs={{0,4},{4,8},{8,12},{12,0},{1,5},{5,9},{9,13},{13,1},{2,6},{6,10},{... | collective-permute-start | bytes 786440 | tf_op jit(solution)/shard_map/ppermute | solution.py:91
  21.9 15.3 %collective-permute-start.1 = (bf16[512,256]{1,0:T(8,128)(2,1)S(1)}, bf16[512,256]{1,0:T(8,128)(2,1)S(1)}, u32[]{:S(2)}, u32[]{:S(2)}) collective-permute-start(bf16[512,256]{1,0:T(8,128)(2,1)S(1)} %collective-permute-done), channel_id=1, source_target_pairs={{0,4},{4,8},{8,12},{12,0},{1,5},{5,9},{9,13},{13,1},{2,6},{6,10},{... | collective-permute-start | bytes 786440 | tf_op jit(solution)/shard_map/ppermute | solution.py:91
  23.1 132.5 %all-reduce.2.cloned.1.call-start = ((), (), s32[]{:S(2)}) async-start(), calls=%async_computation.2 | async-start | bytes 4194304 | tf_op jit(solution)/shard_map/psum | solution.py:118
  37.2 15.2 %collective-permute-start.2 = (bf16[512,256]{1,0:T(8,128)(2,1)S(1)}, bf16[512,256]{1,0:T(8,128)(2,1)S(1)}, u32[]{:S(2)}, u32[]{:S(2)}) collective-permute-start(bf16[512,256]{1,0:T(8,128)(2,1)S(1)} %collective-permute-done.1), channel_id=1, source_target_pairs={{0,4},{4,8},{8,12},{12,0},{1,5},{5,9},{9,13},{13,1},{2,6},{6,10},{... | collective-permute-start | bytes 786440 | tf_op jit(solution)/shard_map/ppermute | solution.py:91
  102.8 1.9 copy-start.2
  104.6 92.7 %reduce-scatter.2.cloned.1.call-start = ((), (), s32[]{:S(2)}) async-start(), calls=%async_computation.3 | async-start | bytes 1310720 | tf_op jit(solution)/shard_map/reduce_scatter | solution.py:134
  104.7 53.4 %copy-start.9 = (f32[1024]{0:T(1024)S(1)}, f32[1024]{0:T(1024)}, u32[]{:S(2)}) copy-start(f32[1024]{0:T(1024)} %param.22) | copy-start | bytes 12292
  155.6 2.4 %copy-start.4 = (bf16[2,1024,256]{2,1,0:T(8,128)(2,1)S(1)}, bf16[2,1024,256]{2,1,0:T(8,128)(2,1)}, u32[]{:S(2)}) copy-start(bf16[2,1024,256]{2,1,0:T(8,128)(2,1)} %param.23) | copy-start | bytes 3145732
  158.6 7.8 %copy-start.7 = (bf16[256,1024]{1,0:T(8,128)(2,1)S(1)}, bf16[256,1024]{1,0:T(8,128)(2,1)}, u32[]{:S(2)}) copy-start(bf16[256,1024]{1,0:T(8,128)(2,1)} %param.27) | copy-start | bytes 1572868
  158.6 7.8 %copy-start.10 = (f32[256]{0:T(256)S(1)}, f32[256]{0:T(256)}, u32[]{:S(2)}) copy-start(f32[256]{0:T(256)} %param.26) | copy-start | bytes 3076
  158.6 7.8 %copy-start.11 = (f32[256]{0:T(256)S(1)}, f32[256]{0:T(256)}, u32[]{:S(2)}) copy-start(f32[256]{0:T(256)} %param.25) | copy-start | bytes 3076
  159.2 5.9 %collective-permute-start.4 = (bf16[15,256]{1,0:T(8,128)(2,1)S(1)}, bf16[15,256]{1,0:T(8,128)(2,1)S(1)}, u32[]{:S(2)}, u32[]{:S(2)}) collective-permute-start(bf16[15,256]{1,0:T(8,128)(2,1)S(1)} %get-tuple-element.126), channel_id=1, source_target_pairs={{4,0},{8,4},{12,8},{5,1},{9,5},{13,9},{6,2},{10,6},{14,10},{7,3},{... | collective-permute-start | bytes 23048 | tf_op jit(solution)/shard_map/ppermute | solution.py:19
  160.5 5.9 %collective-permute-start.3 = (bf16[15,256]{1,0:T(8,128)(2,1)S(1)}, bf16[15,256]{1,0:T(8,128)(2,1)S(1)}, u32[]{:S(2)}, u32[]{:S(2)}) collective-permute-start(bf16[15,256]{1,0:T(8,128)(2,1)S(1)} %get-tuple-element.125), channel_id=1, source_target_pairs={{0,4},{4,8},{8,12},{1,5},{5,9},{9,13},{2,6},{6,10},{10,14},{3,7},{... | collective-permute-start | bytes 23048 | tf_op jit(solution)/shard_map/ppermute | solution.py:16
Sparse Core Ops, SparseCore 0:
  23.2 35.0 all-gather.2
  104.7 50.8 all-reduce.1
  171.4 25.8 reduce-scatter.1
